TPU v7x, 512 devices: a whole 4x8x8 slice. The times are simulated.
512 devices in a mesh: rows: 128 (over z, y, core), grp: 4 (over x).
Axes of the slice: x: 4, y: 8, z: 8, core: 2. Of those that a mesh axis runs over, the one named last changes fastest.
Arguments:
- values: bfloat16 [2048, 64, 256], P(('rows', 'grp'))
- pattern: int32 [2048, 4], P(('rows', 'grp')), may hold values from 0 to 15, as said below
- targets: float32 [131072], P(('rows', 'grp')), may hold values from -6 to 6
- root_weights: float32 [131072], P(('rows', 'grp')), may hold values from 0.25 to 4
Outputs:
- solution: float32 [1024], replicated
- fitted: float32 [131072], P(('rows', 'grp'))
Inputs may be any that keep to these rules, and one draw needn't show every extreme that they name: `pattern`: each tile's 4 entries name distinct column blocks.
All inputs are finite; a program needn't handle non-finite values.
Results may differ from a plain program's by a relative error of at most 0.00035.
Values sent between devices are 32-bit elements; how exact they have to be, the bound alone decides.
A program may use at most 128 MiB of HBM per device.

v0:
```python
import math

import jax
import jax.numpy as jnp
import numpy as np
from jax import lax
from jax.sharding import PartitionSpec as P

NC = 1024
BLK = 64
KB = 4
ITERS = 2
NB = 16


PRECISE = lax.Precision.HIGHEST


def forward(tile_blocks, one_hot, vector):
    lookup_table = vector.reshape(NB, BLK)
    picked = jnp.einsum("tkc,cj->tkj", one_hot, lookup_table, precision=PRECISE)
    result = jnp.einsum(
        "trkj,tkj->tr", tile_blocks, picked, precision=PRECISE, preferred_element_type=jnp.float32
    )
    return result.reshape(-1)


def backward(tile_blocks, one_hot, row_vector):
    row_part = row_vector.reshape(tile_blocks.shape[0], BLK)
    terms = jnp.einsum(
        "trkj,tr->tkj", tile_blocks, row_part, precision=PRECISE, preferred_element_type=jnp.float32
    )
    return jnp.einsum("tkc,tkj->cj", one_hot, terms, precision=PRECISE).reshape(-1)


def solve_lower(lower_factor, vector):
    return jax.scipy.linalg.solve_triangular(lower_factor, vector, lower=True)


def solve_upper(lower_factor, vector):
    return jax.scipy.linalg.solve_triangular(lower_factor, vector, lower=True, trans=1)


def summed_gram(tile_blocks, pattern):
    tile_count = tile_blocks.shape[0]
    selector = (pattern[:, :, None] == jnp.arange(NB, dtype=jnp.int32)[None, None, :]).astype(
        jnp.bfloat16
    )
    dense_rows = jnp.einsum("trkj,tkc->trcj", tile_blocks, selector).reshape(tile_count * BLK, NC)
    local_gram = lax.dot_general(
        dense_rows, dense_rows, (((0,), (0,)), ((), ())), preferred_element_type=jnp.float32
    )
    block_grid = local_gram.reshape(NB, BLK, NB, BLK).transpose(0, 2, 1, 3)
    upper_rows, upper_cols = np.triu_indices(NB)
    halving = np.where(upper_rows == upper_cols, 0.5, 1.0).astype(np.float32)
    packed = block_grid[upper_rows, upper_cols] * jnp.asarray(halving)[:, None, None]
    packed = packed.reshape(upper_rows.shape[0], BLK * BLK)
    summed_pairs = lax.psum(packed, ("rows", "grp"))
    upper_blocks = jnp.zeros((NB, NB, BLK, BLK), jnp.float32)
    upper_blocks = upper_blocks.at[upper_rows, upper_cols].set(summed_pairs.reshape(-1, BLK, BLK))
    full_blocks = upper_blocks + upper_blocks.transpose(1, 0, 3, 2)
    return full_blocks.transpose(0, 2, 1, 3).reshape(NC, NC)


def project(tile_blocks, one_hot, root_weights, p_rows, p_extra, root_ridge, need_back):
    norm_part = lax.psum(jnp.sum(p_rows * p_rows), ("rows", "grp"))
    beta_norm = jnp.sqrt(norm_part + jnp.sum(p_extra * p_extra))
    u_rows = p_rows / beta_norm
    u_extra = p_extra / beta_norm
    back_vec = None
    if need_back:
        local_back = backward(tile_blocks, one_hot, root_weights * u_rows)
        back_vec = lax.psum(local_back, ("rows", "grp")) + root_ridge * u_extra
    return (beta_norm, u_rows, u_extra, back_vec)


def body(values, pattern, targets, root_weights):
    tile_count = values.shape[0]
    tile_blocks = values.reshape(tile_count, BLK, KB, BLK)
    one_hot = (pattern[:, :, None] == jnp.arange(NB, dtype=jnp.int32)[None, None, :]).astype(
        jnp.float32
    )
    gram_total = summed_gram(tile_blocks, pattern)
    rows_total = targets.shape[0] * lax.axis_size("rows") * lax.axis_size("grp")
    ridge_value = rows_total / (2.0 * NC)
    root_ridge = math.sqrt(ridge_value)
    lower_factor = jnp.linalg.cholesky(gram_total + ridge_value * jnp.eye(NC, dtype=jnp.float32))
    scaled = root_weights * targets
    empty_extra = jnp.zeros((NC,), jnp.float32)
    beta_norm, u_rows, u_extra, back_vec = project(
        tile_blocks, one_hot, root_weights, scaled, empty_extra, root_ridge, True
    )
    raw_right = solve_lower(lower_factor, back_vec)
    alpha_norm = jnp.sqrt(jnp.sum(raw_right * raw_right))
    right_vec = raw_right / alpha_norm
    search_dir = right_vec
    phi_bar = beta_norm
    rho_bar = alpha_norm
    iterate = jnp.zeros((NC,), jnp.float32)
    for iteration in range(ITERS):
        is_last = iteration + 1 == ITERS
        lifted = solve_upper(lower_factor, right_vec)
        p_rows = root_weights * forward(tile_blocks, one_hot, lifted) - alpha_norm * u_rows
        p_extra = root_ridge * lifted - alpha_norm * u_extra
        beta_norm, u_rows, u_extra, back_vec = project(
            tile_blocks, one_hot, root_weights, p_rows, p_extra, root_ridge, not is_last
        )
        rho_value = jnp.sqrt(rho_bar * rho_bar + beta_norm * beta_norm)
        cosine = rho_bar / rho_value
        sine_value = beta_norm / rho_value
        phi_value = cosine * phi_bar
        phi_bar = sine_value * phi_bar
        iterate = iterate + phi_value / rho_value * search_dir
        if not is_last:
            raw_right = solve_lower(lower_factor, back_vec) - beta_norm * right_vec
            alpha_norm = jnp.sqrt(jnp.sum(raw_right * raw_right))
            right_vec = raw_right / alpha_norm
            theta_value = sine_value * alpha_norm
            rho_bar = -cosine * alpha_norm
            search_dir = right_vec - theta_value / rho_value * search_dir
    solution = solve_upper(lower_factor, iterate)
    fitted = forward(tile_blocks, one_hot, solution)
    return (solution, fitted)


def solution(mesh):
    in_specs = (
        P(("rows", "grp"), None, None),
        P(("rows", "grp"), None),
        P(("rows", "grp")),
        P(("rows", "grp")),
    )
    out_specs = (P(), P(("rows", "grp")))
    return jax.shard_map(body, mesh=mesh, in_specs=in_specs, out_specs=out_specs, check_vma=False)
```

profile of v0, /device:TPU:1, one launch (start us, length us, event | category | flops | bytes accessed | tf_op | source)
XLA Modules:
  0.0 1082.0 jit_solution(3709175205469957269)
XLA Ops:
  15.1 7.2 gather_fusion
  27.8 5.0 reshape.270
  33.4 107.2 %psum.43 = f32[]{:T(128)} all-reduce(f32[]{:T(128)} %get-tuple-element.93), channel_id=1, replica_groups=mesh['rows'=128,'grp'=4] {'rows','grp'}, use_global_device_ids=true, to_apply=%region_19.20 | all-reduce | flops 1 | bytes 8 | tf_op jit(solution)/shard_map/psum | solution.py:66
  142.3 94.7 %psum.44 = f32[1024]{0:T(1024)S(1)} all-reduce(f32[1024]{0:T(1024)S(1)} %reshape.273), channel_id=1, replica_groups=mesh['rows'=128,'grp'=4] {'rows','grp'}, use_global_device_ids=true, to_apply=%region_20.21 | all-reduce | flops 1024 | bytes 8192 | tf_op jit(solution)/shard_map/psum | solution.py:73
  236.9 87.7 %all-reduce.3.cloned.1.call-done = f32[136,64,64]{2,1,0:T(8,128)} async-done(((f32[136,64,64]{2,1,0:T(8,128)}), f32[136,64,64]{2,1,0:T(8,128)}) %all-reduce.3.cloned.1.call-update) | async-done | bytes 2228240 | tf_op jit(solution)/shard_map/psum | solution.py:58
  328.9 23.1 %scatter_fusion = f32[16,16,64,64]{3,2,1,0:T(8,128)} fusion(f32[16,16,64,64]{3,2,1,0:T(8,128)} %broadcast_in_dim.12, s32[136]{0:T(256)S(1)} %copy-done, f32[136,64,64]{2,1,0:T(8,128)} %all-reduce.3.cloned.1.call-done), kind=kCustom, calls=%fused_computation.1 | custom fusion | bytes 6685760 | tf_op jit(solution)/shard_map/scatter | solution.py:60
  352.0 9.3 copy.41
  361.3 12.0 %fusion = f32[16,64,16,64]{3,1,2,0:T(8,128)} fusion(f32[16,16,64,64]{3,2,1,0:T(8,128)} %scatter_fusion, f32[16,16,64,64]{2,3,0,1:T(8,128)} %copy.41), kind=kLoop, calls=%fused_computation.5 | loop fusion | flops 1048576 | bytes 12582912 | tf_op jit(solution)/shard_map/transpose | solution.py:62
  373.3 9.8 copy.42
  383.1 7.6 reshape.271
  390.7 4.8 select_add_fusion
  395.5 5.5 copy.43
  407.4 11.7 %cholesky.222 = f32[128,128]{1,0:T(8,128)S(1)} custom-call(f32[128,128]{1,0:T(8,128)S(1)} %cholesky.577), custom_call_target="Cholesky" | custom-call | tf_op jit(solution)/shard_map/jit(cholesky)/cholesky | solution.py:87
  419.2 9.8 custom-call.65
  432.1 11.7 %cholesky.243 = f32[128,128]{1,0:T(8,128)S(1)} custom-call(f32[128,128]{1,0:T(8,128)S(1)} %cholesky.581), custom_call_target="Cholesky" | custom-call | tf_op jit(solution)/shard_map/jit(cholesky)/cholesky | solution.py:87
  447.2 9.8 custom-call.66
  462.5 11.7 %cholesky.466 = f32[128,128]{1,0:T(8,128)S(1)} custom-call(f32[128,128]{1,0:T(8,128)S(1)} %cholesky.586), custom_call_target="Cholesky" | custom-call | tf_op jit(solution)/shard_map/jit(cholesky)/cholesky | solution.py:87
  475.0 9.8 custom-call.67
  489.3 11.7 %cholesky.485 = f32[128,128]{1,0:T(8,128)S(1)} custom-call(f32[128,128]{1,0:T(8,128)S(1)} %cholesky.591), custom_call_target="Cholesky" | custom-call | tf_op jit(solution)/shard_map/jit(cholesky)/cholesky | solution.py:87
  501.8 9.8 custom-call.68
  516.0 11.9 %cholesky.504 = f32[128,128]{1,0:T(8,128)S(1)} custom-call(f32[128,128]{1,0:T(8,128)S(1)} %cholesky.596), custom_call_target="Cholesky" | custom-call | tf_op jit(solution)/shard_map/jit(cholesky)/cholesky | solution.py:87
  528.6 9.8 custom-call.69
  542.7 11.7 %cholesky.524 = f32[128,128]{1,0:T(8,128)S(1)} custom-call(f32[128,128]{1,0:T(8,128)S(1)} %cholesky.601), custom_call_target="Cholesky" | custom-call | tf_op jit(solution)/shard_map/jit(cholesky)/cholesky | solution.py:87
  555.1 9.8 custom-call.70
  569.0 11.7 %cholesky.544 = f32[128,128]{1,0:T(8,128)S(1)} custom-call(f32[128,128]{1,0:T(8,128)S(1)} %cholesky.606), custom_call_target="Cholesky" | custom-call | tf_op jit(solution)/shard_map/jit(cholesky)/cholesky | solution.py:87
  581.5 9.8 custom-call.71
  594.3 11.7 %cholesky.562 = f32[128,128]{1,0:T(8,128)S(1)} custom-call(f32[128,128]{1,0:T(8,128)S(1)} %convolution_subtract_fusion.6), custom_call_target="Cholesky" | custom-call | tf_op jit(solution)/shard_map/jit(cholesky)/cholesky | solution.py:87
  621.3 23.9 %while.10 = (s32[]{:T(128)}, f32[1024,1024]{0,1:T(8,128)}, s32[8,2]{0,1:T(2,128)S(1)}, f32[8,128,128]{2,1,0:T(8,128)S(1)}, s32[]{:T(128)}) while((s32[]{:T(128)}, f32[1024,1024]{0,1:T(8,128)}, s32[8,2]{0,1:T(2,128)S(1)}, f32[8,128,128]{2,1,0:T(8,128)S(1)}, s32[]{:T(128)}) %tuple.112), condition=%wide.while_cond.1.clone.1, body=%wide.while_body.1.clone.1.sunk | while | flops 2 | bytes 393321 | solution.py:41
  645.1 78.8 %custom-call.83 = f32[8,128,128]{1,2,0:T(8,128)S(1)} custom-call(f32[8,128,128]{2,1,0:T(8,128)S(1)} %get-tuple-element.42), custom_call_target="InvertDiagBlocksLowerTriangular" | custom-call | tf_op jit(solution)/shard_map/jit(_solve_triangular)/triangular_solve | solution.py:41
  748.0 97.3 %psum.45 = f32[]{:T(128)} all-reduce(f32[]{:T(128)} %get-tuple-element.91), channel_id=1, replica_groups=mesh['rows'=128,'grp'=4] {'rows','grp'}, use_global_device_ids=true, to_apply=%region_23.26 | all-reduce | flops 1 | bytes 8 | tf_op jit(solution)/shard_map/psum | solution.py:66
  847.3 95.1 %psum.46 = f32[1024]{0:T(1024)S(1)} all-reduce(f32[1024]{0:T(1024)S(1)} %reshape.277), channel_id=1, replica_groups=mesh['rows'=128,'grp'=4] {'rows','grp'}, use_global_device_ids=true, to_apply=%region_25.28 | all-reduce | flops 1024 | bytes 8192 | tf_op jit(solution)/shard_map/psum | solution.py:73
  966.7 94.4 %psum.47 = f32[]{:T(128)} all-reduce(f32[]{:T(128)} %multiply_reduce_fusion.4), channel_id=1, replica_groups=mesh['rows'=128,'grp'=4] {'rows','grp'}, use_global_device_ids=true, to_apply=%region_28.31 | all-reduce | flops 1 | bytes 8 | tf_op jit(solution)/shard_map/psum | solution.py:66
  (299 shorter events, 154.2 us)
Async XLA Ops:
  7.2 317.5 %all-reduce.3.cloned.1.call-start = ((), (), s32[]{:S(2)}) async-start(), calls=%async_computation | async-start | bytes 8912896 | tf_op jit(solution)/shard_map/psum | solution.py:58
  10.6 4.5 copy-start
  22.3 3.7 copy-start.4
  27.8 5.0 copy-start.2
  27.8 5.0 copy-start.5
  405.5 1.9 copy-start.1
  1073.7 1.2 copy-start.3
Sparse Core Ops, SparseCore 0:
  32.9 291.7 all-reduce.2
where the time goes:
time: 1090 us; the launch traced here: 1080 us
  blocking collectives  489 us (45%)
  other arithmetic  278 us (26%)
  local copies, waits for them, and re-layouts  115 us (11%)
  waiting for transfers between devices  87.8 us (8%)
  matrix products  86.2 us (8%)
  between operations  25.5 us (2%)
    psum x3, blocking collectives, project(): norm_part = lax.psum(jnp.sum(p_rows * p_rows), ('rows', 'grp'))  299 us
    psum x2, blocking collectives, project(): back_vec = lax.psum(local_back, ('rows', 'grp')) + root_ridge * u_extra  190 us
    another operation x30, other arithmetic, body(): jnp.linalg.cholesky(gram_total + ridge_value * jnp.eye(NC, dtype=jnp.floa...  167 us
    psum x1, waiting for transfers between devices, summed_gram(): summed_pairs = lax.psum(packed, ('rows', 'grp'))  87.7 us
    another operation x4, other arithmetic, solve_upper(): jax.scipy.linalg.solve_triangular(lower_factor, vector, lower=True, trans=1)  83.6 us
    scatter x2, local copies, waits for them, and re-layouts, summed_gram(): upper_blocks.at[upper_rows, upper_cols]  32.4 us
    another operation x45, matrix products, solve_upper(): jax.scipy.linalg.solve_triangular(lower_factor, vector, lower=True, trans=1)  32 us
    another operation x14, matrix products, body(): jnp.linalg.cholesky(gram_total + ridge_value * jnp.eye(NC, dtype=jnp.floa...  27.2 us
  transfers between devices with their start and end apart: 1, of which 1 were waited for; matrix products, arithmetic and copies ran while one was open for 0% of the time, Pallas kernels for 0%

commit v1 on v0

v1 whole, which is shorter than its diff:
```python
import jax
import jax.numpy as jnp
from jax import lax
from jax.experimental import pallas as pl
from jax.experimental.pallas import tpu as pltpu
from jax.sharding import PartitionSpec as P

NC = 1024
BLK = 64
KB = 4
B = 128
NB = NC // B
WIDTH = KB * BLK
TOL = 2e-6
CHECK = 2e-5
LIMIT = 300
ROUNDS = 4
DOUBLINGS = 5
STEPS = 9
CONTRACT_LANES = (((1,), (1,)), ((), ()))
MESH = pl.DeviceIdType.MESH

NEAR = [(i, d) for i in range(NB // 2) for d in range(NB // 2)]
PAIRS = [(4 * c + i, (4 * c + i + d) % NB) for c in range(2) for i, d in NEAR]
PAIRS = PAIRS[:16] + [(0, 4), (1, 5)] + PAIRS[16:] + [(6, 2), (7, 3)]
PER_CORE = len(PAIRS) // 2
INDEX = {pair: n for n, pair in enumerate(PAIRS)}

NZ, NY, NX = 8, 8, 4
HALF = PER_CORE * B
PART_A, PART_B, PART_C = 0, 512, 1024
SLAB = 512 // NZ
CELL = SLAB // NY
WIDE = (HALF - PART_C) // NX
SIDE = 192
THIN1 = SIDE // NY
THIN2 = (WIDE - SIDE) // NZ


def split2(x):
    hi = x.astype(jnp.bfloat16)
    return hi, (x - hi.astype(jnp.float32)).astype(jnp.bfloat16)


def split3(x):
    hi = x.astype(jnp.bfloat16)
    mid, lo = split2(x - hi.astype(jnp.float32))
    return hi, mid, lo


def dot_nt(x, y):
    return lax.dot_general(x, y, CONTRACT_LANES, preferred_element_type=jnp.float32)


def stacked(row):
    parts = [part.astype(jnp.float32) for part in split3(row)]
    line = lax.broadcasted_iota(jnp.int32, (16, row.shape[1]), 0)
    value = jnp.where(line == 0, parts[0], 0.0)
    value = jnp.where(line == 1, parts[1], value)
    return jnp.where(line == 2, parts[2], value).astype(jnp.bfloat16)


def pack(rows):
    line = lax.broadcasted_iota(jnp.int32, (NB, B), 0)
    value = jnp.where(line == 0, rows[0], 0.0)
    for j in range(1, NB):
        value = jnp.where(line == j, rows[j], value)
    return value


def dense_block(values, columns, dense_t, lanes):
    rows = lax.broadcasted_iota(jnp.int32, (NC, WIDTH), 0).astype(jnp.float32)
    first = lax.broadcasted_iota(jnp.int32, (NC, B), 1) < BLK
    for half in range(2):
        pair = values[half].astype(jnp.bfloat16)
        picks = [
            jnp.where(rows == columns[n : n + 1, :], 1.0, 0.0).astype(jnp.bfloat16)
            for n in (2 * half, 2 * half + 1)
        ]
        both = jnp.where(first, dot_nt(picks[0], pair), dot_nt(picks[1], pair))
        start = lanes + half * B
        dense_t[:NC, start : start + B] = both.astype(jnp.bfloat16)


def remote(src, dst, send, recv, device):
    moved = pltpu.make_async_remote_copy(
        src_ref=src, dst_ref=dst, send_sem=send, recv_sem=recv, device_id=device, device_id_type=MESH
    )
    moved.start()
    return moved


def greet(peers):
    barrier = pltpu.get_barrier_semaphore()
    for peer in peers:
        pl.semaphore_signal(barrier, inc=1, device_id=peer, device_id_type=MESH)
    return barrier


def position():
    place = lax.axis_index("rows")
    return place, lax.axis_index("grp"), place % 2, (place // 2) % NY, place // (2 * NY)


def reduce_kernel(
    ridge, values_in, pattern_in, targets_in, weights_in, operator, own_dense, mat, inverse, side, begin,
    values, pattern, targets, weights, raw, extra, there, extra_there, dense_t, gathered_m, columns, load_sem,
    send_raw, recv_raw, *rest,
):
    place, x, core, y, z = position()
    loads = [
        pltpu.make_async_copy(source, target, load_sem.at[n])
        for n, (source, target) in enumerate(
            ((values_in, values), (pattern_in, pattern), (targets_in, targets), (weights_in, weights))
        )
    ]
    for item in loads:
        item.start()

    def along_z(d):
        return (((z + d) % NZ) * 2 * NY + y * 2 + core, x)

    def along_y(d):
        return (z * 2 * NY + ((y + d) % NY) * 2 + core, x)

    def along_x(d):
        return (place, (x + d) % NX)

    sibling = (place + 1 - 2 * core, x)
    peers = [sibling]
    peers += [along_z(d) for d in range(1, NZ)] + [along_y(d) for d in range(1, NY)]
    peers += [along_x(d) for d in range(1, NX)]
    barrier = greet(peers)
    for item in loads:
        item.wait()
    raw[...] = values[...].astype(jnp.float32)
    lane = lax.broadcasted_iota(jnp.int32, (1, WIDTH), 1)
    for n in range(4):
        block = jnp.where(lane < BLK, pattern[n : n + 1, 0:1], pattern[n : n + 1, 1:2])
        after = jnp.where(lane < 3 * BLK, pattern[n : n + 1, 2:3], pattern[n : n + 1, 3:4])
        block = jnp.where(lane < 2 * BLK, block, after)
        extra[n : n + 1, :] = (block * BLK + lane % BLK).astype(jnp.float32)
    square = weights[...] * weights[...]
    extra[4:5, :] = square
    extra[5:6, :] = square * targets[...]
    extra[6:8, :] = jnp.zeros((2, WIDTH), jnp.float32)
    pl.semaphore_wait(barrier, len(peers))

    first = remote(raw, there, send_raw.at[0], recv_raw.at[0], sibling)
    second = remote(extra, extra_there, send_raw.at[1], recv_raw.at[1], sibling)
    dense_block(values, extra, dense_t, 0)
    own_dense[...] = dense_t[:NC, :WIDTH]
    first.wait()
    second.wait()
    dense_block(there, extra_there, dense_t, WIDTH)

    dense_t[NC:, :] = dense_t[: NC // 2, :]
    own = 4 * core

    def make_blocks(local, product):
        for i in range(NB // 2):
            start = pl.multiple_of((own + i) * B, B)
            block = product(start, start, 4 * B)
            for d in range(4):
                row = (4 * i + d) * B
                local[row : row + B, :] = block[:, d * B : (d + 1) * B]
        for i in range(2):
            start = pl.multiple_of((6 * core + i) * B, B)
            row = (16 + i) * B
            local[row : row + B, :] = product(start, pl.multiple_of(start + 4 * B, B), B)

    def plain(first, second, count):
        return dot_nt(dense_t[pl.ds(first, B), :], dense_t[pl.ds(second, count), :])

    square = jnp.concatenate([extra[4:5, :], extra_there[4:5, :]], axis=1)

    def weighted(first, second, count):
        hi, lo = split2(dense_t[pl.ds(first, B), :].astype(jnp.float32) * square)
        others = dense_t[pl.ds(second, count), :]
        return dot_nt(hi, others) + dot_nt(lo, others)

    def rows(start, count):
        return pl.ds(pl.multiple_of(start, 8), count)

    def total(mine, arrived):
        value = mine
        for n in range(arrived.shape[0]):
            value = value + arrived[n]
        return value

    def ordered(slots):
        value = slots[0]
        for n in range(1, slots.shape[0]):
            value = value + slots[n]
        return value

    sent = []

    def scatter(axis, source, start, count, landing, send, recv, base):
        step, me, size = axis
        out = []
        for d in range(1, size):
            target = (me + d) % size
            piece = source.at[rows(start + target * count, count)]
            out.append(remote(piece, landing.at[d - 1], send.at[base + d - 1], recv.at[base + d - 1], step(d)))
        sent.extend(out)
        return out

    def spread(axis, source, landing, send, recv, base):
        step, _, size = axis
        out = []
        for d in range(1, size):
            out.append(remote(source, landing, send.at[base + d - 1], recv.at[base + d - 1], step(d)))
        sent.extend(out)
        return out

    def arrive(copies):
        for item in copies:
            item.wait_recv()

    axis_z, axis_y, axis_x = (along_z, z, NZ), (along_y, y, NY), (along_x, x, NX)
    half = core * HALF

    def job(refs, result):
        local, in_a, in_b, in_c, slab_a, slab_b, wide_c, in_a2, in_b2, in_c1, in_c2, in_cells, in_thin1, in_thin2 = refs[:14]
        send1, recv1, send2, recv2, send3, recv3, send4, recv4, send5, recv5, send6, recv6 = refs[14:]

        def place_of(start, count):
            return result.at[rows(half + start, count)]

        c1 = scatter(axis_x, local, PART_C, WIDE, in_c, send1, recv1, 0)
        a1 = scatter(axis_z, local, PART_A, SLAB, in_a, send1, recv1, 3)
        b1 = scatter(axis_y, local, PART_B, SLAB, in_b, send1, recv1, 10)
        yield
        arrive(a1)
        slab_a[...] = total(local[rows(PART_A + z * SLAB, SLAB), :], in_a)
        a2 = scatter(axis_y, slab_a, 0, CELL, in_a2, send2, recv2, 0)
        arrive(b1)
        slab_b[...] = total(local[rows(PART_B + y * SLAB, SLAB), :], in_b)
        b2 = scatter(axis_z, slab_b, 0, CELL, in_b2, send2, recv2, 7)
        arrive(c1)
        wide_c[...] = total(local[rows(PART_C + x * WIDE, WIDE), :], in_c)
        d2 = scatter(axis_y, wide_c, 0, THIN1, in_c1, send2, recv2, 14)
        e2 = scatter(axis_z, wide_c, SIDE, THIN2, in_c2, send2, recv2, 21)
        yield
        arrive(a2)
        in_cells[x, :CELL, :] = total(slab_a[rows(y * CELL, CELL), :], in_a2)
        arrive(b2)
        in_cells[x, CELL:, :] = total(slab_b[rows(z * CELL, CELL), :], in_b2)
        ab3 = spread(axis_x, in_cells.at[x], in_cells.at[x], send3, recv3, 0)
        arrive(d2)
        in_thin1[z] = total(wide_c[rows(y * THIN1, THIN1), :], in_c1)
        d3 = spread(axis_z, in_thin1.at[z], in_thin1.at[z], send3, recv3, 3)
        arrive(e2)
        in_thin2[y] = total(wide_c[rows(SIDE + z * THIN2, THIN2), :], in_c2)
        e3 = spread(axis_y, in_thin2.at[y], in_thin2.at[y], send3, recv3, 10)
        yield
        cell_a = place_of(PART_A + z * SLAB + y * CELL, CELL)
        cell_b = place_of(PART_B + y * SLAB + z * CELL, CELL)
        thin_d = place_of(PART_C + x * WIDE + y * THIN1, THIN1)
        thin_e = place_of(PART_C + x * WIDE + SIDE + z * THIN2, THIN2)
        arrive(ab3)
        both = ordered(in_cells)
        cell_a[...] = both[:CELL]
        cell_b[...] = both[CELL:]
        a4 = spread(axis_y, cell_a, cell_a, send4, recv4, 0)
        b4 = spread(axis_z, cell_b, cell_b, send4, recv4, 7)
        arrive(d3)
        thin_d[...] = ordered(in_thin1)
        d4 = spread(axis_y, thin_d, thin_d, send4, recv4, 14)
        arrive(e3)
        thin_e[...] = ordered(in_thin2)
        e4 = spread(axis_z, thin_e, thin_e, send4, recv4, 21)
        yield
        big_a, big_b = place_of(PART_A + z * SLAB, SLAB), place_of(PART_B + y * SLAB, SLAB)
        big_c = place_of(PART_C + x * WIDE, WIDE)
        arrive(d4)
        arrive(e4)
        c5 = spread(axis_x, big_c, big_c, send5, recv5, 0)
        arrive(a4)
        a5 = spread(axis_z, big_a, big_a, send5, recv5, 3)
        arrive(b4)
        b5 = spread(axis_y, big_b, big_b, send5, recv5, 10)
        yield

        def across(start, count, n):
            block = place_of(start, count)
            item = remote(block, block, send6.at[n], recv6.at[n], sibling)
            sent.append(item)
            return item

        arrive(a5)
        last = [across(PART_A, PART_B - PART_A, 0)]
        arrive(b5)
        last.append(across(PART_B, PART_C - PART_B, 1))
        arrive(c5)
        last.append(across(PART_C, HALF - PART_C, 2))
        yield
        arrive(last)
        yield

    count = len(rest) // 2
    locals_m, locals_w = rest[:count], rest[count:]
    make_blocks(locals_m[0], plain)
    aims = stacked(jnp.concatenate([extra[5:6, :], extra_there[5:6, :]], axis=1))
    for c in range(NC // BLK):
        line = dot_nt(aims, dense_t[c * BLK : (c + 1) * BLK, :])
        locals_m[0][BLK + c : BLK + c + 1, :BLK] = jnp.sum(line, axis=0, keepdims=True)
    job_m = job(locals_m, gathered_m)
    next(job_m)
    make_blocks(locals_w[0], weighted)
    job_w = job(locals_w, operator)
    next(job_w)
    for _ in range(4):
        next(job_m)
        next(job_w)
    next(job_m)
    next(job_m)

    unpack(ridge, gathered_m, mat, side)
    invert_blocks(mat, inverse)
    next(job_w)
    begin[...] = first_steps(mat, inverse, columns, side[...])
    next(job_w)
    for item in sent:
        item.wait_send()


def diagonal():
    shape = (B, B)
    return lax.broadcasted_iota(jnp.int32, shape, 0) == lax.broadcasted_iota(jnp.int32, shape, 1)


def to_row(column):
    return jnp.sum(jnp.where(diagonal(), column, 0.0), axis=0, keepdims=True)


def to_column(row):
    return jnp.sum(jnp.where(diagonal(), row, 0.0), axis=1, keepdims=True)


def dot(x, y):
    return jnp.sum(jnp.sum(x * y, axis=0, keepdims=True), axis=1, keepdims=True)


def block_rows(block, column):
    return jnp.sum((block * column).reshape(B // 8, 8, B), axis=0)


def spread_columns(vector, columns):
    for j in range(NB):
        columns[j] = jnp.broadcast_to(to_column(vector[j : j + 1, :]), (B, B))


def apply_full(mat, columns):
    acc = [None] * NB
    for i in range(NB):
        column = columns[i]
        for j in range(NB):
            part = block_rows(mat[i, j], column)
            acc[j] = part if acc[j] is None else acc[j] + part
    return pack([jnp.sum(part, axis=0, keepdims=True) for part in acc])


def apply_diag(inverse, vector, columns):
    rows = []
    for b in range(NB):
        column = jnp.sum(inverse[b] * vector[b : b + 1, :], axis=1, keepdims=True)
        column = jnp.broadcast_to(column, (B, B))
        columns[b] = column
        rows.append(to_row(column))
    return pack(rows)


def invert_blocks(mat, inverse):
    identity = diagonal()
    one = jnp.where(identity, 1.0, 0.0)
    upper = lax.broadcasted_iota(jnp.int32, (B, B), 0) < BLK
    left = lax.broadcasted_iota(jnp.int32, (B, B), 1) < BLK
    errors, scales = [], []
    for b in range(NB):
        block = jnp.where(upper == left, mat[b, b], 0.0)
        middle = jnp.where(identity, block, 0.0)
        row = lax.rsqrt(jnp.sum(middle, axis=0, keepdims=True))
        column = lax.rsqrt(jnp.sum(middle, axis=1, keepdims=True))
        block = block * row * column
        bound = jnp.max(jnp.sum(jnp.abs(block), axis=1, keepdims=True), axis=0, keepdims=True)
        errors.append(one - block / bound)
        scales.append(row * column / bound)

    def times(rows, square):
        (top, rest), (hi, lo) = split2(rows), split2(square)
        both = jnp.dot(top, hi, preferred_element_type=jnp.float32)
        both = both + jnp.dot(rest, hi, preferred_element_type=jnp.float32)
        return both + jnp.dot(top, lo, preferred_element_type=jnp.float32)

    sums = [one + error for error in errors]
    errors = [times(error, error) for error in errors]
    for n in range(DOUBLINGS):
        for b in range(NB):
            if n + 1 == DOUBLINGS:
                sums[b] = sums[b] + times(sums[b], errors[b])
            else:
                both = times(jnp.concatenate([errors[b], sums[b]], axis=0), errors[b])
                errors[b] = both[:B]
                sums[b] = sums[b] + both[B:]
    for b in range(NB):
        inverse[b] = sums[b] * scales[b]


def eliminate(mat, spare, right, columns, out):
    spare[...] = mat[...]
    spread_columns(right, columns)
    lane = lax.broadcasted_iota(jnp.int32, (B, B), 1)
    line = lax.broadcasted_iota(jnp.int32, (B, B), 0)

    def pivot(k, carry):
        kb, kr = k // B, k % B
        rows = [spare[kb, j, pl.ds(kr, 1), :] for j in range(NB)]
        entry = columns[kb, pl.ds(kr, 1), :]
        value = jnp.sum(jnp.where(lane[:1] == kr, spare[kb, kb, pl.ds(kr, 1), :], 0.0), axis=1, keepdims=True)

        def sweep(i, carry):
            factor = jnp.sum(jnp.where(lane == kr, spare[i, kb], 0.0), axis=1, keepdims=True) / value
            factor = jnp.where((line == kr) & (i == kb), 0.0, factor)
            for j in range(NB):
                spare[i, j] = spare[i, j] - factor * rows[j]
            columns[i] = columns[i] - factor * entry
            return carry

        return lax.fori_loop(0, NB, sweep, carry)

    lax.fori_loop(0, NC, pivot, 0)
    rows = []
    for b in range(NB):
        scale = jnp.sum(jnp.where(diagonal(), spare[b, b], 0.0), axis=1, keepdims=True)
        rows.append(to_row(columns[b] / scale))
    out[...] = pack(rows)


def first_steps(mat, inverse, columns, right):
    zero = jnp.zeros((NB, B), jnp.float32)
    pre = apply_diag(inverse, right, columns)
    size = dot(right, pre)
    bound = (TOL * TOL) * size
    image = apply_full(mat, columns)

    def advance(_, carry):
        res, pre, image, step, moved, total, size, ratio, length = carry
        step = pre + ratio * step
        moved = image + ratio * moved
        total = total + length * step
        res = res - length * moved
        pre = apply_diag(inverse, res, columns)
        latest = dot(res, pre)
        image = apply_full(mat, columns)
        active = latest > bound
        ratio = jnp.where(active, latest / size, 0.0)
        further = jnp.where(active, latest / (dot(image, pre) - ratio * latest / length), 0.0)
        return res, pre, image, step, moved, total, latest, ratio, further

    start = (right, pre, image, zero, zero, zero, size, jnp.zeros((1, 1), jnp.float32), size / dot(image, pre))
    carry = lax.fori_loop(0, STEPS - 1, advance, start)
    res, pre, image, step, moved, total, size, ratio, length = carry
    return total + length * (pre + ratio * step)


def solve(mat, inverse, spare, columns, right, out, begin=None):
    zero = jnp.zeros((NB, B), jnp.float32)

    def inner(res, pre, size, bound):
        image = apply_full(mat, columns)

        def going(carry):
            return (carry[0] < LIMIT) & (carry[1] > bound)

        def advance(carry):
            count, _, res, pre, image, step, moved, total, size, ratio, length = carry
            step = pre + ratio * step
            moved = image + ratio * moved
            total = total + length * step
            res = res - length * moved
            pre = apply_diag(inverse, res, columns)
            latest = dot(res, pre)
            image = apply_full(mat, columns)
            ratio = latest / size
            length = latest / (dot(image, pre) - ratio * latest / length)
            return count + 1, latest[0, 0], res, pre, image, step, moved, total, latest, ratio, length

        start = (
            jnp.int32(0), size[0, 0], res, pre, image, zero, zero, zero,
            size, jnp.zeros((1, 1), jnp.float32), size / dot(image, pre),
        )
        return lax.while_loop(going, advance, start)[7]

    def residual(value):
        spread_columns(value, columns)
        res = right - apply_full(mat, columns)
        pre = apply_diag(inverse, res, columns)
        return res, pre, dot(res, pre)

    pre = apply_diag(inverse, right, columns)
    size = dot(right, pre)
    first = size[0, 0]
    if begin is None:
        out[...] = zero
        begun = (jnp.int32(0), first, right, pre, size)
    else:
        out[...] = begin
        res, pre, size = residual(begin)
        begun = (jnp.int32(0), size[0, 0], res, pre, size)

    def unsolved(carry):
        return (carry[0] < ROUNDS) & (carry[1] > CHECK * CHECK * first)

    def improve(carry):
        count, _, res, pre, size = carry
        out[...] += inner(res, pre, size, TOL * TOL * first)
        res, pre, size = residual(out[...])
        return count + 1, size[0, 0], res, pre, size

    final = lax.while_loop(unsolved, improve, begun)[1]

    @pl.when(jnp.logical_not(final <= CHECK * CHECK * first))
    def _():
        eliminate(mat, spare, right, columns, out)


def corner_fixed(block):
    low = lax.broadcasted_iota(jnp.int32, (B, B), 0) >= BLK
    low = low & (lax.broadcasted_iota(jnp.int32, (B, B), 1) < BLK)
    return jnp.where(low, block.T, block)


def unpack(ridge, grams, mat, side):
    identity = diagonal()
    left = lax.broadcasted_iota(jnp.int32, (1, B), 1) < BLK
    sides = []
    for j in range(NB):
        even = grams[BLK + 2 * j : BLK + 2 * j + 1, :]
        odd = grams[BLK + 2 * j + 1 : BLK + 2 * j + 2, :]
        sides.append(jnp.where(left, even, pltpu.roll(odd, BLK, 1)))
    side[...] = pack(sides)
    for n, (i, j) in enumerate(PAIRS):
        block = grams[n * B : (n + 1) * B, :]
        if n % PER_CORE == 0:
            block = corner_fixed(block)
        if i == j:
            mat[i, i] = block + jnp.where(identity, ridge, 0.0)
        else:
            mat[i, j] = block
            mat[j, i] = block.T


def apply_operator(blocks, ridge, vector, columns):
    spread_columns(vector, columns)
    down = [jnp.zeros((8, B), jnp.float32)] * NB
    rows = []
    for i in range(NB):
        column = columns[i]
        across = jnp.zeros((B, B), jnp.float32)
        for j in range(NB):
            if (i, j) in INDEX:
                block = blocks[INDEX[i, j]]
                down[j] = down[j] + block_rows(block, column)
                if j != i:
                    across = across + block * vector[j : j + 1, :]
        rows.append(to_row(jnp.sum(across, axis=1, keepdims=True)))
    total = [jnp.sum(part, axis=0, keepdims=True) + row for part, row in zip(down, rows)]
    return pack(total) + ridge * vector


def solver_kernel(ridge, blocks, dense_t, mat, inverse, side, begin, solution, fitted, spare, columns, first, second):
    g = side[...]
    solve(mat, inverse, spare, columns, g, first, begin[...])
    z = first[...]
    h = apply_operator(blocks, ridge, z, columns)
    gain = dot(g, z)
    length = gain / dot(z, h)
    rest = g - length * h
    solve(mat, inverse, spare, columns, rest, second)
    s = second[...]
    latest = dot(rest, s)
    ratio = latest / gain
    image = apply_operator(blocks, ridge, s, columns) + ratio * h
    step = s + ratio * z
    curve = dot(step, image)
    x = length * z + jnp.where(curve > 0.0, latest / curve, 0.0) * step
    solution[...] = x

    spread_columns(x, columns)
    for half in range(2):
        acc = jnp.zeros((8, B), jnp.float32)
        for j in range(NB):
            part = dense_t[j * B : (j + 1) * B, half * B : (half + 1) * B].astype(jnp.float32)
            acc = acc + block_rows(part, columns[j])
        fitted[half : half + 1, :] = jnp.sum(acc, axis=0, keepdims=True)


def space(*shape):
    return pltpu.VMEM(shape, jnp.float32)


def shaped(*shape):
    return jax.ShapeDtypeStruct(shape, jnp.float32)


WHOLE = pl.BlockSpec(memory_space=pltpu.VMEM)
LIMITS = dict(vmem_limit_bytes=32 << 20)


def body(values, pattern, targets, root_weights):
    tiles = values.shape[0]
    own_rows = tiles * BLK
    rows_total = own_rows * lax.axis_size("rows") * lax.axis_size("grp")
    ridge = rows_total / (2.0 * NC)
    job_space = [
        space(HALF, B),
        space(NZ - 1, SLAB, B),
        space(NY - 1, SLAB, B),
        space(NX - 1, WIDE, B),
        space(SLAB, B),
        space(SLAB, B),
        space(WIDE, B),
        space(NY - 1, CELL, B),
        space(NZ - 1, CELL, B),
        space(NY - 1, THIN1, B),
        space(NZ - 1, THIN2, B),
        space(NX, 2 * CELL, B),
        space(NZ, THIN1, B),
        space(NY, THIN2, B),
    ] + [pltpu.SemaphoreType.DMA((n,)) for n in (17, 17, 28, 28, 17, 17, 28, 28, 17, 17, 3, 3)]
    operator, dense_t, mat, inverse, side, begin = pl.pallas_call(
        lambda *refs: reduce_kernel(ridge, *refs),
        out_shape=(
            shaped(2 * HALF, B),
            jax.ShapeDtypeStruct((NC, own_rows), jnp.bfloat16),
            shaped(NB, NB, B, B),
            shaped(NB, B, B),
            shaped(NB, B),
            shaped(NB, B),
        ),
        in_specs=[pl.BlockSpec(memory_space=pltpu.HBM)] * 4,
        out_specs=(WHOLE,) * 6,
        scratch_shapes=[
            pltpu.VMEM((2, B, WIDTH), jnp.bfloat16),
            pltpu.VMEM(pattern.shape, jnp.int32),
            space(1, WIDTH),
            space(1, WIDTH),
            space(2, B, WIDTH),
            space(8, WIDTH),
            space(2, B, WIDTH),
            space(8, WIDTH),
            pltpu.VMEM((NC + NC // 2, 2 * WIDTH), jnp.bfloat16),
            space(2 * HALF, B),
            space(NB, B, B),
            pltpu.SemaphoreType.DMA((4,)),
            pltpu.SemaphoreType.DMA((2,)),
            pltpu.SemaphoreType.DMA((2,)),
        ]
        + job_space * 2,
        compiler_params=pltpu.CompilerParams(collective_id=0, has_side_effects=True, **LIMITS),
    )(
        *(
            pltpu.with_memory_space_constraint(operand, pltpu.HBM)
            for operand in (
                values.reshape(tiles // 2, 2 * BLK, WIDTH), pattern, targets.reshape(1, -1), root_weights.reshape(1, -1)
            )
        )
    )
    solution_rows, fitted = pl.pallas_call(
        lambda *refs: solver_kernel(ridge, *refs),
        out_shape=(shaped(NB, B), shaped(own_rows // B, B)),
        in_specs=[WHOLE] * 6,
        out_specs=(WHOLE,) * 2,
        scratch_shapes=[space(NB, NB, B, B), space(NB, B, B), space(NB, B), space(NB, B)],
        compiler_params=pltpu.CompilerParams(**LIMITS),
    )(operator.reshape(len(PAIRS), B, B), dense_t, mat, inverse, side, begin)
    return solution_rows.reshape(-1), fitted.reshape(-1)


def solution(mesh):
    in_specs = (
        P(("rows", "grp"), None, None),
        P(("rows", "grp"), None),
        P(("rows", "grp")),
        P(("rows", "grp")),
    )
    out_specs = (P(), P(("rows", "grp")))
    return jax.shard_map(body, mesh=mesh, in_specs=in_specs, out_specs=out_specs, check_vma=False)
```

time: 1090 us -> 85.7 us (0.08)
  blocking collectives: 489 us -> 0 us
  other arithmetic: 278 us -> 0 us
  local copies, waits for them, and re-layouts: 115 us -> 0 us
  waiting for transfers between devices: 87.8 us -> 0 us
  matrix products: 86.2 us -> 0 us
  Pallas kernels: 0 us -> 84.9 us
  between operations: 25.5 us -> 0.64 us
    psum x5 -> x0, blocking collectives: 489 us -> none  [the longest x3 299 us: project(): norm_part = lax.psum(jnp.sum(p_rows * p_rows), ('rows', 'grp'))]
    another operation x34 -> x0, other arithmetic: 251 us -> none  [the longest x30 167 us: body(): jnp.linalg.cholesky(gram_total + ridge_value * jnp.eye(NC, dtype=jnp.floa...]
    psum x1 -> x0, waiting for transfers between devices: 87.7 us -> none  [summed_gram(): summed_pairs = lax.psum(packed, ('rows', 'grp'))]
    pallas_call x0 -> x2, Pallas kernels: none -> 84.9 us  [the longest x1 75 us: body(): pl.pallas_call(lambda *refs: reduce_kernel(ridge, *refs), out_shape=(shap...]
    another operation x89 -> x0, matrix products: 79 us -> none  [the longest x45 32 us: solve_upper(): jax.scipy.linalg.solve_triangular(lower_factor, vector, lower=True, trans=1)]
    another operation x78 -> x0, local copies, waits for them, and re-layouts: 32.5 us -> none  [the longest x53 23.7 us: solve_upper(): jax.scipy.linalg.solve_triangular(lower_factor, vector, lower=True, trans=1)]
    scatter x2 -> x0, local copies, waits for them, and re-layouts: 32.4 us -> none  [summed_gram(): upper_blocks.at[upper_rows, upper_cols]]
    reshape x15 -> x0, local copies, waits for them, and re-layouts: 15.9 us -> none  [the longest x1 7.62 us: summed_gram(): return full_blocks.transpose(0, 2, 1, 3).reshape(NC, NC)]
  transfers between devices with their start and end apart: 1 -> 0, of which waited for: 1 -> 0; matrix products, arithmetic and copies ran while one was open for 0% -> 0% of each run, Pallas kernels for 0% -> 0%
where the time goes in v1:
time: 85.7 us; the launch traced here: 85.5 us
  Pallas kernels  84.9 us (99%)
    pallas_call x1, Pallas kernels, body(): pl.pallas_call(lambda *refs: reduce_kernel(ridge, *refs), out_shape=(shap...  75 us
    pallas_call x1, Pallas kernels, body(): pl.pallas_call(lambda *refs: solver_kernel(ridge, *refs), out_shape=(shap...  9.9 us

profile of v1, /device:TPU:1, one launch (start us, length us, event | category | flops | bytes accessed | tf_op | source)
XLA Modules:
  0.0 85.5 jit_solution(14145680034164939444)
XLA Ops:
  0.6 75.0 %shard_map.59 = (f32[4608,128]{1,0:T(8,128)S(1)}, bf16[1024,256]{1,0:T(8,128)(2,1)S(1)}, f32[8,8,128,128]{3,2,1,0:T(8,128)S(1)}, f32[8,128,128]{2,1,0:T(8,128)S(...) custom-call(bf16[2,128,256]{2,1,0:T(8,128)(2,1)} %bitcast.7, s32[4,4]{1,0:T(4,128)} %refs_1_.1, f32[1,256]{1,0:T(1,128)} %bitcast.8, ...), custom_call_target="tpu_custom_call" | custom-call | tf_op jit(solution)/shard_map/pallas_call | solution.py:633
  75.6 9.9 %shard_map.60 = (f32[8,128]{1,0:T(8,128)}, f32[2,128]{1,0:T(2,128)}) custom-call(f32[36,128,128]{2,1,0:T(8,128)S(1)} %bitcast.6, bf16[1024,256]{1,0:T(8,128)(2,1)S(1)} %get-tuple-element.11.refs_1_, f32[8,8,128,128]{3,2,1,0:T(8,128)S(1)} %get-tuple-element.12.refs_2_, f32[8,128,128]{2,1,0:T(8,128)S(1)} %get-tuple-element.13.refs_3_, ...), custom_call_target="tpu_custom_call" | custom-call | tf_op jit(solution)/shard_map/pallas_call | solution.py:671

commit v2 on v1

--- a/solution.py
+++ b/solution.py
@@ -103,7 +103,7 @@
 
 
 def reduce_kernel(
-    ridge, values_in, pattern_in, targets_in, weights_in, operator, own_dense, mat, inverse, side, begin,
+    ridge, values_in, pattern_in, targets_in, weights_in, operator, own_dense, mat, inverse, side, begin, left,
     values, pattern, targets, weights, raw, extra, there, extra_there, dense_t, gathered_m, columns, load_sem,
     send_raw, recv_raw, *rest,
 ):
@@ -157,13 +157,15 @@
     dense_t[NC:, :] = dense_t[: NC // 2, :]
     own = 4 * core
 
-    def make_blocks(local, product):
-        for i in range(NB // 2):
+    def near_blocks(local, product, which):
+        for i in which:
             start = pl.multiple_of((own + i) * B, B)
             block = product(start, start, 4 * B)
             for d in range(4):
                 row = (4 * i + d) * B
                 local[row : row + B, :] = block[:, d * B : (d + 1) * B]
+
+    def far_blocks(local, product):
         for i in range(2):
             start = pl.multiple_of((6 * core + i) * B, B)
             row = (16 + i) * B
@@ -194,136 +196,162 @@
             value = value + slots[n]
         return value
 
-    sent = []
-
-    def scatter(axis, source, start, count, landing, send, recv, base):
+    def settle(ref, sem):
+        pltpu.make_async_copy(ref, ref, sem).wait()
+
+    def scatter(axis, piece, landing, send, recv):
         step, me, size = axis
-        out = []
         for d in range(1, size):
-            target = (me + d) % size
-            piece = source.at[rows(start + target * count, count)]
-            out.append(remote(piece, landing.at[d - 1], send.at[base + d - 1], recv.at[base + d - 1], step(d)))
-        sent.extend(out)
-        return out
-
-    def spread(axis, source, landing, send, recv, base):
+            remote(piece((me + d) % size), landing.at[d - 1], send, recv, step(d))
+
+    def spread(axis, block, send, recv):
         step, _, size = axis
-        out = []
         for d in range(1, size):
-            out.append(remote(source, landing, send.at[base + d - 1], recv.at[base + d - 1], step(d)))
-        sent.extend(out)
-        return out
-
-    def arrive(copies):
-        for item in copies:
-            item.wait_recv()
+            remote(block, block, send, recv, step(d))
 
     axis_z, axis_y, axis_x = (along_z, z, NZ), (along_y, y, NY), (along_x, x, NX)
     half = core * HALF
 
-    def job(refs, result):
-        local, in_a, in_b, in_c, slab_a, slab_b, wide_c, in_a2, in_b2, in_c1, in_c2, in_cells, in_thin1, in_thin2 = refs[:14]
-        send1, recv1, send2, recv2, send3, recv3, send4, recv4, send5, recv5, send6, recv6 = refs[14:]
+    def job(refs, result, product, finish):
+        local, in_a, in_b, in_c, mix_y, mix_z, in_y, in_z, in_cells, in_thin1, in_thin2, out_y, out_z, send, recv = refs
+        sizes = []
+
+        def sems(count):
+            sizes.append(count)
+            return send.at[len(sizes) - 1], recv.at[len(sizes) - 1]
 
         def place_of(start, count):
             return result.at[rows(half + start, count)]
 
-        c1 = scatter(axis_x, local, PART_C, WIDE, in_c, send1, recv1, 0)
-        a1 = scatter(axis_z, local, PART_A, SLAB, in_a, send1, recv1, 3)
-        b1 = scatter(axis_y, local, PART_B, SLAB, in_b, send1, recv1, 10)
+        def part(start, count):
+            return lambda k: local.at[rows(start + k * count, count)]
+
+        near_blocks(local, product, (2, 3))
+        far_blocks(local, product)
+        sem_c = sems((NX - 1) * WIDE)
+        scatter(axis_x, part(PART_C, WIDE), in_c, *sem_c)
+        near_blocks(local, product, (1,))
+        sem_b = sems((NY - 1) * SLAB)
+        scatter(axis_y, part(PART_B, SLAB), in_b, *sem_b)
+        near_blocks(local, product, (0,))
+        finish(local)
+        sem_a = sems((NZ - 1) * SLAB)
+        scatter(axis_z, part(PART_A, SLAB), in_a, *sem_a)
         yield
-        arrive(a1)
-        slab_a[...] = total(local[rows(PART_A + z * SLAB, SLAB), :], in_a)
-        a2 = scatter(axis_y, slab_a, 0, CELL, in_a2, send2, recv2, 0)
-        arrive(b1)
-        slab_b[...] = total(local[rows(PART_B + y * SLAB, SLAB), :], in_b)
-        b2 = scatter(axis_z, slab_b, 0, CELL, in_b2, send2, recv2, 7)
-        arrive(c1)
-        wide_c[...] = total(local[rows(PART_C + x * WIDE, WIDE), :], in_c)
-        d2 = scatter(axis_y, wide_c, 0, THIN1, in_c1, send2, recv2, 14)
-        e2 = scatter(axis_z, wide_c, SIDE, THIN2, in_c2, send2, recv2, 21)
+        settle(in_a, sem_a[1])
+        slab = total(local[rows(PART_A + z * SLAB, SLAB), :], in_a)
+        for k in range(NY):
+            mix_y[k, :CELL, :] = slab[k * CELL : (k + 1) * CELL]
+        settle(in_b, sem_b[1])
+        slab = total(local[rows(PART_B + y * SLAB, SLAB), :], in_b)
+        for k in range(NZ):
+            mix_z[k, :CELL, :] = slab[k * CELL : (k + 1) * CELL]
+        settle(in_c, sem_c[1])
+        slab = total(local[rows(PART_C + x * WIDE, WIDE), :], in_c)
+        for k in range(NY):
+            mix_y[k, CELL:, :] = slab[k * THIN1 : (k + 1) * THIN1]
+        for k in range(NZ):
+            mix_z[k, CELL:, :] = slab[SIDE + k * THIN2 : SIDE + (k + 1) * THIN2]
+        sem_y, sem_z = sems((NY - 1) * (CELL + THIN1)), sems((NZ - 1) * (CELL + THIN2))
+        scatter(axis_y, lambda k: mix_y.at[k], in_y, *sem_y)
+        scatter(axis_z, lambda k: mix_z.at[k], in_z, *sem_z)
         yield
-        arrive(a2)
-        in_cells[x, :CELL, :] = total(slab_a[rows(y * CELL, CELL), :], in_a2)
-        arrive(b2)
-        in_cells[x, CELL:, :] = total(slab_b[rows(z * CELL, CELL), :], in_b2)
-        ab3 = spread(axis_x, in_cells.at[x], in_cells.at[x], send3, recv3, 0)
-        arrive(d2)
-        in_thin1[z] = total(wide_c[rows(y * THIN1, THIN1), :], in_c1)
-        d3 = spread(axis_z, in_thin1.at[z], in_thin1.at[z], send3, recv3, 3)
-        arrive(e2)
-        in_thin2[y] = total(wide_c[rows(SIDE + z * THIN2, THIN2), :], in_c2)
-        e3 = spread(axis_y, in_thin2.at[y], in_thin2.at[y], send3, recv3, 10)
+        settle(in_y, sem_y[1])
+        mixed = total(mix_y[y], in_y)
+        in_cells[x, :CELL, :] = mixed[:CELL]
+        in_thin1[z] = mixed[CELL:]
+        sem_1 = sems((NZ - 1) * THIN1)
+        spread(axis_z, in_thin1.at[z], *sem_1)
+        settle(in_z, sem_z[1])
+        mixed = total(mix_z[z], in_z)
+        in_cells[x, CELL:, :] = mixed[:CELL]
+        in_thin2[y] = mixed[CELL:]
+        sem_2, sem_3 = sems((NY - 1) * THIN2), sems((NX - 1) * 2 * CELL)
+        spread(axis_y, in_thin2.at[y], *sem_2)
+        spread(axis_x, in_cells.at[x], *sem_3)
         yield
-        cell_a = place_of(PART_A + z * SLAB + y * CELL, CELL)
-        cell_b = place_of(PART_B + y * SLAB + z * CELL, CELL)
-        thin_d = place_of(PART_C + x * WIDE + y * THIN1, THIN1)
-        thin_e = place_of(PART_C + x * WIDE + SIDE + z * THIN2, THIN2)
-        arrive(ab3)
+        settle(in_cells.at[pl.ds(0, NX - 1)], sem_3[1])
         both = ordered(in_cells)
-        cell_a[...] = both[:CELL]
-        cell_b[...] = both[CELL:]
-        a4 = spread(axis_y, cell_a, cell_a, send4, recv4, 0)
-        b4 = spread(axis_z, cell_b, cell_b, send4, recv4, 7)
-        arrive(d3)
-        thin_d[...] = ordered(in_thin1)
-        d4 = spread(axis_y, thin_d, thin_d, send4, recv4, 14)
-        arrive(e3)
-        thin_e[...] = ordered(in_thin2)
-        e4 = spread(axis_z, thin_e, thin_e, send4, recv4, 21)
+        settle(in_thin1.at[pl.ds(0, NZ - 1)], sem_1[1])
+        out_y[y, :CELL, :] = both[:CELL]
+        out_y[y, CELL:, :] = ordered(in_thin1)
+        sem_y = sems((NY - 1) * (CELL + THIN1))
+        spread(axis_y, out_y.at[y], *sem_y)
+        settle(in_thin2.at[pl.ds(0, NY - 1)], sem_2[1])
+        out_z[z, :CELL, :] = both[CELL:]
+        out_z[z, CELL:, :] = ordered(in_thin2)
+        sem_z = sems((NZ - 1) * (CELL + THIN2))
+        spread(axis_z, out_z.at[z], *sem_z)
         yield
         big_a, big_b = place_of(PART_A + z * SLAB, SLAB), place_of(PART_B + y * SLAB, SLAB)
         big_c = place_of(PART_C + x * WIDE, WIDE)
-        arrive(d4)
-        arrive(e4)
-        c5 = spread(axis_x, big_c, big_c, send5, recv5, 0)
-        arrive(a4)
-        a5 = spread(axis_z, big_a, big_a, send5, recv5, 3)
-        arrive(b4)
-        b5 = spread(axis_y, big_b, big_b, send5, recv5, 10)
+        settle(out_y.at[pl.ds(0, NY - 1)], sem_y[1])
+        settle(out_z.at[pl.ds(0, NZ - 1)], sem_z[1])
+        big_c[:SIDE, :] = out_y[:, CELL:, :].reshape(SIDE, B)
+        big_c[SIDE:, :] = out_z[:, CELL:, :].reshape(WIDE - SIDE, B)
+        sem_c = sems((NX - 1) * WIDE)
+        spread(axis_x, big_c, *sem_c)
+        big_a[...] = out_y[:, :CELL, :].reshape(SLAB, B)
+        sem_a = sems((NZ - 1) * SLAB)
+        spread(axis_z, big_a, *sem_a)
+        big_b[...] = out_z[:, :CELL, :].reshape(SLAB, B)
+        sem_b = sems((NY - 1) * SLAB)
+        spread(axis_y, big_b, *sem_b)
         yield
-
-        def across(start, count, n):
+        across = []
+        for start, count, (_, arrived) in (
+            (PART_A, PART_B - PART_A, sem_a), (PART_B, PART_C - PART_B, sem_b), (PART_C, HALF - PART_C, sem_c)
+        ):
+            settle(local.at[pl.ds(0, sizes_of(start))], arrived)
+            pair = sems(count)
             block = place_of(start, count)
-            item = remote(block, block, send6.at[n], recv6.at[n], sibling)
-            sent.append(item)
-            return item
-
-        arrive(a5)
-        last = [across(PART_A, PART_B - PART_A, 0)]
-        arrive(b5)
-        last.append(across(PART_B, PART_C - PART_B, 1))
-        arrive(c5)
-        last.append(across(PART_C, HALF - PART_C, 2))
+            remote(block, block, *pair, sibling)
+            across.append((block, pair[1]))
         yield
-        arrive(last)
+        for block, arrived in across:
+            settle(block, arrived)
         yield
+        for n, moved in enumerate(sizes):
+            settle(local.at[pl.ds(0, moved)], send.at[n])
+        yield
+
+    def sizes_of(start):
+        return {PART_A: (NZ - 1) * SLAB, PART_B: (NY - 1) * SLAB, PART_C: (NX - 1) * WIDE}[start]
 
     count = len(rest) // 2
     locals_m, locals_w = rest[:count], rest[count:]
-    make_blocks(locals_m[0], plain)
     aims = stacked(jnp.concatenate([extra[5:6, :], extra_there[5:6, :]], axis=1))
-    for c in range(NC // BLK):
-        line = dot_nt(aims, dense_t[c * BLK : (c + 1) * BLK, :])
-        locals_m[0][BLK + c : BLK + c + 1, :BLK] = jnp.sum(line, axis=0, keepdims=True)
-    job_m = job(locals_m, gathered_m)
+
+    def add_side(local):
+        for c in range(NC // BLK):
+            line = dot_nt(aims, dense_t[c * BLK : (c + 1) * BLK, :])
+            local[BLK + c : BLK + c + 1, :BLK] = jnp.sum(line, axis=0, keepdims=True)
+
+    job_m = job(locals_m, gathered_m, plain, add_side)
+    job_w = job(locals_w, operator, weighted, lambda local: None)
     next(job_m)
-    make_blocks(locals_w[0], weighted)
-    job_w = job(locals_w, operator)
     next(job_w)
     for _ in range(4):
         next(job_m)
         next(job_w)
     next(job_m)
+    unpack(ridge, gathered_m, mat, core)
     next(job_m)
-
-    unpack(ridge, gathered_m, mat, side)
+    unpack(ridge, gathered_m, mat, 1 - core)
+    side[...] = right_side(gathered_m)
+
     invert_blocks(mat, inverse)
+    advance, finish, state = first_steps(mat, inverse, columns, side[...])
+    state = lax.fori_loop(0, STEPS // 2, advance, state)
     next(job_w)
-    begin[...] = first_steps(mat, inverse, columns, side[...])
+    state = lax.fori_loop(STEPS // 2, STEPS - 1, advance, state)
+    value = finish(state)
+    begin[...] = value
+    spread_columns(value, columns)
+    left[...] = side[...] - apply_full(mat, columns)
     next(job_w)
-    for item in sent:
-        item.wait_send()
+    next(job_m)
+    next(job_w)
 
 
 def diagonal():
@@ -459,13 +487,15 @@
         further = jnp.where(active, latest / (dot(image, pre) - ratio * latest / length), 0.0)
         return res, pre, image, step, moved, total, latest, ratio, further
 
+    def finish(carry):
+        _, pre, _, step, _, total, _, ratio, length = carry
+        return total + length * (pre + ratio * step)
+
     start = (right, pre, image, zero, zero, zero, size, jnp.zeros((1, 1), jnp.float32), size / dot(image, pre))
-    carry = lax.fori_loop(0, STEPS - 1, advance, start)
-    res, pre, image, step, moved, total, size, ratio, length = carry
-    return total + length * (pre + ratio * step)
-
-
-def solve(mat, inverse, spare, columns, right, out, begin=None):
+    return advance, finish, start
+
+
+def solve(mat, inverse, spare, columns, right, out, given=None, least=0.0):
     zero = jnp.zeros((NB, B), jnp.float32)
 
     def inner(res, pre, size, bound):
@@ -500,14 +530,15 @@
         return res, pre, dot(res, pre)
 
     pre = apply_diag(inverse, right, columns)
-    size = dot(right, pre)
-    first = size[0, 0]
-    if begin is None:
+    whole = dot(right, pre)
+    first = jnp.maximum(whole[0, 0], least)
+    if given is None:
         out[...] = zero
-        begun = (jnp.int32(0), first, right, pre, size)
+        begun = (jnp.int32(0), whole[0, 0], right, pre, whole)
     else:
-        out[...] = begin
-        res, pre, size = residual(begin)
+        out[...], res = given
+        pre = apply_diag(inverse, res, columns)
+        size = dot(res, pre)
         begun = (jnp.int32(0), size[0, 0], res, pre, size)
 
     def unsolved(carry):
@@ -525,6 +556,8 @@
     def _():
         eliminate(mat, spare, right, columns, out)
 
+    return first
+
 
 def corner_fixed(block):
     low = lax.broadcasted_iota(jnp.int32, (B, B), 0) >= BLK
@@ -532,20 +565,28 @@
     return jnp.where(low, block.T, block)
 
 
-def unpack(ridge, grams, mat, side):
-    identity = diagonal()
+def right_side(grams):
     left = lax.broadcasted_iota(jnp.int32, (1, B), 1) < BLK
     sides = []
     for j in range(NB):
         even = grams[BLK + 2 * j : BLK + 2 * j + 1, :]
         odd = grams[BLK + 2 * j + 1 : BLK + 2 * j + 2, :]
         sides.append(jnp.where(left, even, pltpu.roll(odd, BLK, 1)))
-    side[...] = pack(sides)
-    for n, (i, j) in enumerate(PAIRS):
-        block = grams[n * B : (n + 1) * B, :]
-        if n % PER_CORE == 0:
+    return pack(sides)
+
+
+def unpack(ridge, grams, mat, core):
+    identity = diagonal()
+    for n in range(PER_CORE):
+        block = grams[pl.ds(pl.multiple_of(core * HALF + n * B, B), B), :]
+        if n == 0:
             block = corner_fixed(block)
-        if i == j:
+        if n < 16:
+            i, d = 4 * core + n // 4, n % 4
+        else:
+            i, d = 6 * core + n - 16, 4
+        j = (i + d) % NB
+        if d == 0:
             mat[i, i] = block + jnp.where(identity, ridge, 0.0)
         else:
             mat[i, j] = block
@@ -570,15 +611,15 @@
     return pack(total) + ridge * vector
 
 
-def solver_kernel(ridge, blocks, dense_t, mat, inverse, side, begin, solution, fitted, spare, columns, first, second):
+def solver_kernel(ridge, blocks, dense_t, mat, inverse, side, begin, left, solution, fitted, spare, columns, first, second):
     g = side[...]
-    solve(mat, inverse, spare, columns, g, first, begin[...])
+    least = solve(mat, inverse, spare, columns, g, first, (begin[...], left[...]))
     z = first[...]
     h = apply_operator(blocks, ridge, z, columns)
     gain = dot(g, z)
     length = gain / dot(z, h)
     rest = g - length * h
-    solve(mat, inverse, spare, columns, rest, second)
+    solve(mat, inverse, spare, columns, rest, second, least=least)
     s = second[...]
     latest = dot(rest, s)
     ratio = latest / gain
@@ -614,23 +655,23 @@
     own_rows = tiles * BLK
     rows_total = own_rows * lax.axis_size("rows") * lax.axis_size("grp")
     ridge = rows_total / (2.0 * NC)
+    groups = 3 + 2 + 3 + 2 + 3 + 3
     job_space = [
         space(HALF, B),
         space(NZ - 1, SLAB, B),
         space(NY - 1, SLAB, B),
         space(NX - 1, WIDE, B),
-        space(SLAB, B),
-        space(SLAB, B),
-        space(WIDE, B),
-        space(NY - 1, CELL, B),
-        space(NZ - 1, CELL, B),
-        space(NY - 1, THIN1, B),
-        space(NZ - 1, THIN2, B),
+        space(NY, CELL + THIN1, B),
+        space(NZ, CELL + THIN2, B),
+        space(NY - 1, CELL + THIN1, B),
+        space(NZ - 1, CELL + THIN2, B),
         space(NX, 2 * CELL, B),
         space(NZ, THIN1, B),
         space(NY, THIN2, B),
-    ] + [pltpu.SemaphoreType.DMA((n,)) for n in (17, 17, 28, 28, 17, 17, 28, 28, 17, 17, 3, 3)]
-    operator, dense_t, mat, inverse, side, begin = pl.pallas_call(
+        space(NY, CELL + THIN1, B),
+        space(NZ, CELL + THIN2, B),
+    ] + [pltpu.SemaphoreType.DMA((groups,))] * 2
+    operator, dense_t, mat, inverse, side, begin, left = pl.pallas_call(
         lambda *refs: reduce_kernel(ridge, *refs),
         out_shape=(
             shaped(2 * HALF, B),
@@ -639,9 +680,10 @@
             shaped(NB, B, B),
             shaped(NB, B),
             shaped(NB, B),
+            shaped(NB, B),
         ),
         in_specs=[pl.BlockSpec(memory_space=pltpu.HBM)] * 4,
-        out_specs=(WHOLE,) * 6,
+        out_specs=(WHOLE,) * 7,
         scratch_shapes=[
             pltpu.VMEM((2, B, WIDTH), jnp.bfloat16),
             pltpu.VMEM(pattern.shape, jnp.int32),
@@ -671,11 +713,11 @@
     solution_rows, fitted = pl.pallas_call(
         lambda *refs: solver_kernel(ridge, *refs),
         out_shape=(shaped(NB, B), shaped(own_rows // B, B)),
-        in_specs=[WHOLE] * 6,
+        in_specs=[WHOLE] * 7,
         out_specs=(WHOLE,) * 2,
         scratch_shapes=[space(NB, NB, B, B), space(NB, B, B), space(NB, B), space(NB, B)],
         compiler_params=pltpu.CompilerParams(**LIMITS),
-    )(operator.reshape(len(PAIRS), B, B), dense_t, mat, inverse, side, begin)
+    )(operator.reshape(len(PAIRS), B, B), dense_t, mat, inverse, side, begin, left)
     return solution_rows.reshape(-1), fitted.reshape(-1)
 
 

time: 85.7 us -> 82 us (0.957)
  Pallas kernels: 84.9 us -> 81.2 us
    pallas_call x1, Pallas kernels: 75 us -> 72.3 us  [body(): pl.pallas_call(lambda *refs: reduce_kernel(ridge, *refs), out_shape=(shap...]
    pallas_call x1, Pallas kernels: 9.9 us -> 8.86 us  [body(): pl.pallas_call(lambda *refs: solver_kernel(ridge, *refs), out_shape=(shap...]
where the time goes in v2:
time: 82 us; the launch traced here: 81.8 us
  Pallas kernels  81.2 us (99%)
    pallas_call x1, Pallas kernels, body(): pl.pallas_call(lambda *refs: reduce_kernel(ridge, *refs), out_shape=(shap...  72.3 us
    pallas_call x1, Pallas kernels, body(): pl.pallas_call(lambda *refs: solver_kernel(ridge, *refs), out_shape=(shap...  8.86 us

profile of v2, /device:TPU:1, one launch (start us, length us, event | category | flops | bytes accessed | tf_op | source)
XLA Modules:
  0.0 81.8 jit_solution(9613378356001483494)
XLA Ops:
  0.6 72.3 %shard_map.59 = (f32[4608,128]{1,0:T(8,128)S(1)}, bf16[1024,256]{1,0:T(8,128)(2,1)S(1)}, f32[8,8,128,128]{3,2,1,0:T(8,128)S(1)}, f32[8,128,128]{2,1,0:T(8,128)S(...) custom-call(bf16[2,128,256]{2,1,0:T(8,128)(2,1)} %bitcast.7, s32[4,4]{1,0:T(4,128)} %refs_1_.1, ...), custom_call_target="tpu_custom_call" | custom-call | tf_op jit(solution)/shard_map/pallas_call | solution.py:674
  73.0 8.9 %shard_map.60 = (f32[8,128]{1,0:T(8,128)}, f32[2,128]{1,0:T(2,128)}) custom-call(f32[36,128,128]{2,1,0:T(8,128)S(1)} %bitcast.6, bf16[1024,256]{1,0:T(8,128)(2,1)S(1)} %get-tuple-element.12.refs_1_, f32[8,8,128,128]{3,2,1,0:T(8,128)S(1)} %get-tuple-element.13.refs_2_, f32[8,128,128]{2,1,0:T(8,128)S(1)} %get-tuple-element.14.refs_3_, ...), custom_call_target="tpu_custom_call" | custom-call | tf_op jit(solution)/shard_map/pallas_call | solution.py:713

commit v3 on v2

--- a/solution.py
+++ b/solution.py
@@ -11,12 +11,12 @@
 B = 128
 NB = NC // B
 WIDTH = KB * BLK
-TOL = 2e-6
+TOL = 5e-6
 CHECK = 2e-5
 LIMIT = 300
 ROUNDS = 4
 DOUBLINGS = 5
-STEPS = 9
+STEPS = 8
 CONTRACT_LANES = (((1,), (1,)), ((), ()))
 MESH = pl.DeviceIdType.MESH
 
@@ -212,8 +212,8 @@
     axis_z, axis_y, axis_x = (along_z, z, NZ), (along_y, y, NY), (along_x, x, NX)
     half = core * HALF
 
-    def job(refs, result, product, finish):
-        local, in_a, in_b, in_c, mix_y, mix_z, in_y, in_z, in_cells, in_thin1, in_thin2, out_y, out_z, send, recv = refs
+    def job(refs, result, product, finish, late):
+        local, in_a, in_b, in_c, relay, pass_on, mix_y, mix_z, in_y, in_z, in_cells, in_thin1, in_thin2, out_y, out_z, send, recv = refs
         sizes = []
 
         def sems(count):
@@ -226,17 +226,51 @@
         def part(start, count):
             return lambda k: local.at[rows(start + k * count, count)]
 
-        near_blocks(local, product, (2, 3))
-        far_blocks(local, product)
-        sem_c = sems((NX - 1) * WIDE)
-        scatter(axis_x, part(PART_C, WIDE), in_c, *sem_c)
-        near_blocks(local, product, (1,))
-        sem_b = sems((NY - 1) * SLAB)
-        scatter(axis_y, part(PART_B, SLAB), in_b, *sem_b)
-        near_blocks(local, product, (0,))
-        finish(local)
+        def opposite():
+            out = [sems(WIDE // 2) for _ in range(4)]
+            left, right, across = (x + NX - 1) % NX, (x + 1) % NX, (x + 2) % NX
+            middle = WIDE // 2
+            far = PART_C + across * WIDE
+            remote(local.at[rows(far, middle)], relay.at[0], *out[0], along_x(1))
+            remote(local.at[rows(far + middle, middle)], relay.at[1], *out[1], along_x(NX - 1))
+            near = PART_C + right * WIDE + middle
+            remote(local.at[rows(near, middle)], in_c.at[0, pl.ds(middle, middle)], *out[2], along_x(1))
+            near = PART_C + left * WIDE
+            remote(local.at[rows(near, middle)], in_c.at[1, pl.ds(0, middle)], *out[3], along_x(NX - 1))
+            return out
+
+        def relayed(out):
+            left, right, middle = (x + NX - 1) % NX, (x + 1) % NX, WIDE // 2
+            more = [sems(middle) for _ in range(2)]
+            settle(relay.at[0], out[0][1])
+            pass_on[0] = relay[0] + local[rows(PART_C + right * WIDE, middle), :]
+            remote(pass_on.at[0], in_c.at[0, pl.ds(0, middle)], *more[0], along_x(1))
+            settle(relay.at[1], out[1][1])
+            pass_on[1] = relay[1] + local[rows(PART_C + left * WIDE + middle, middle), :]
+            remote(pass_on.at[1], in_c.at[1, pl.ds(middle, middle)], *more[1], along_x(NX - 1))
+            return out[2:] + more
+
+        if late:
+            near_blocks(local, product, (0, 1, 2, 3))
+            far_blocks(local, product)
+            finish(local)
+            yield
+            by_x = opposite()
+            sem_b = sems((NY - 1) * SLAB)
+            scatter(axis_y, part(PART_B, SLAB), in_b, *sem_b)
+        else:
+            near_blocks(local, product, (2, 3))
+            far_blocks(local, product)
+            by_x = opposite()
+            near_blocks(local, product, (1,))
+            sem_b = sems((NY - 1) * SLAB)
+            scatter(axis_y, part(PART_B, SLAB), in_b, *sem_b)
+            near_blocks(local, product, (0,))
+            finish(local)
         sem_a = sems((NZ - 1) * SLAB)
         scatter(axis_z, part(PART_A, SLAB), in_a, *sem_a)
+        yield
+        by_x = relayed(by_x)
         yield
         settle(in_a, sem_a[1])
         slab = total(local[rows(PART_A + z * SLAB, SLAB), :], in_a)
@@ -246,7 +280,8 @@
         slab = total(local[rows(PART_B + y * SLAB, SLAB), :], in_b)
         for k in range(NZ):
             mix_z[k, :CELL, :] = slab[k * CELL : (k + 1) * CELL]
-        settle(in_c, sem_c[1])
+        for n, pair in enumerate(by_x):
+            settle(relay.at[n % 2], pair[1])
         slab = total(local[rows(PART_C + x * WIDE, WIDE), :], in_c)
         for k in range(NY):
             mix_y[k, CELL:, :] = slab[k * THIN1 : (k + 1) * THIN1]
@@ -289,8 +324,13 @@
         settle(out_z.at[pl.ds(0, NZ - 1)], sem_z[1])
         big_c[:SIDE, :] = out_y[:, CELL:, :].reshape(SIDE, B)
         big_c[SIDE:, :] = out_z[:, CELL:, :].reshape(WIDE - SIDE, B)
-        sem_c = sems((NX - 1) * WIDE)
-        spread(axis_x, big_c, *sem_c)
+        middle = WIDE // 2
+        firsts, seconds = [sems(middle) for _ in range(2)], [sems(middle) for _ in range(2)]
+        upper, lower = place_of(PART_C + x * WIDE, middle), place_of(PART_C + x * WIDE + middle, middle)
+        remote(upper, upper, *firsts[0], along_x(1))
+        remote(lower, lower, *firsts[1], along_x(NX - 1))
+        remote(lower, lower, *seconds[0], along_x(1))
+        remote(upper, upper, *seconds[1], along_x(NX - 1))
         big_a[...] = out_y[:, :CELL, :].reshape(SLAB, B)
         sem_a = sems((NZ - 1) * SLAB)
         spread(axis_z, big_a, *sem_a)
@@ -298,11 +338,22 @@
         sem_b = sems((NY - 1) * SLAB)
         spread(axis_y, big_b, *sem_b)
         yield
+        forward = [sems(middle) for _ in range(2)]
+        from_left = place_of(PART_C + ((x + NX - 1) % NX) * WIDE, middle)
+        from_right = place_of(PART_C + ((x + 1) % NX) * WIDE + middle, middle)
+        settle(from_left, firsts[0][1])
+        remote(from_left, from_left, *forward[0], along_x(1))
+        settle(from_right, firsts[1][1])
+        remote(from_right, from_right, *forward[1], along_x(NX - 1))
+        yield
         across = []
-        for start, count, (_, arrived) in (
-            (PART_A, PART_B - PART_A, sem_a), (PART_B, PART_C - PART_B, sem_b), (PART_C, HALF - PART_C, sem_c)
+        for start, count, size, waits in (
+            (PART_A, PART_B - PART_A, (NZ - 1) * SLAB, [sem_a]),
+            (PART_B, PART_C - PART_B, (NY - 1) * SLAB, [sem_b]),
+            (PART_C, HALF - PART_C, middle, seconds + forward),
         ):
-            settle(local.at[pl.ds(0, sizes_of(start))], arrived)
+            for _, arrived in waits:
+                settle(local.at[pl.ds(0, size)], arrived)
             pair = sems(count)
             block = place_of(start, count)
             remote(block, block, *pair, sibling)
@@ -315,9 +366,6 @@
             settle(local.at[pl.ds(0, moved)], send.at[n])
         yield
 
-    def sizes_of(start):
-        return {PART_A: (NZ - 1) * SLAB, PART_B: (NY - 1) * SLAB, PART_C: (NX - 1) * WIDE}[start]
-
     count = len(rest) // 2
     locals_m, locals_w = rest[:count], rest[count:]
     aims = stacked(jnp.concatenate([extra[5:6, :], extra_there[5:6, :]], axis=1))
@@ -327,24 +375,21 @@
             line = dot_nt(aims, dense_t[c * BLK : (c + 1) * BLK, :])
             local[BLK + c : BLK + c + 1, :BLK] = jnp.sum(line, axis=0, keepdims=True)
 
-    job_m = job(locals_m, gathered_m, plain, add_side)
-    job_w = job(locals_w, operator, weighted, lambda local: None)
-    next(job_m)
-    next(job_w)
-    for _ in range(4):
-        next(job_m)
-        next(job_w)
-    next(job_m)
+    job_m = job(locals_m, gathered_m, plain, add_side, False)
+    job_w = job(locals_w, operator, weighted, lambda local: None, True)
+    for turn in "mwmww" + "mw" * 3 + "mmwmw":
+        next(job_m if turn == "m" else job_w)
     unpack(ridge, gathered_m, mat, core)
+    invert_blocks(mat, inverse, 4 * core)
     next(job_m)
     unpack(ridge, gathered_m, mat, 1 - core)
     side[...] = right_side(gathered_m)
 
-    invert_blocks(mat, inverse)
+    invert_blocks(mat, inverse, 4 - 4 * core)
     advance, finish, state = first_steps(mat, inverse, columns, side[...])
-    state = lax.fori_loop(0, STEPS // 2, advance, state)
+    state = lax.fori_loop(0, 2, advance, state)
     next(job_w)
-    state = lax.fori_loop(STEPS // 2, STEPS - 1, advance, state)
+    state = lax.fori_loop(2, STEPS - 1, advance, state)
     value = finish(state)
     begin[...] = value
     spread_columns(value, columns)
@@ -400,14 +445,14 @@
     return pack(rows)
 
 
-def invert_blocks(mat, inverse):
+def invert_blocks(mat, inverse, start):
     identity = diagonal()
     one = jnp.where(identity, 1.0, 0.0)
     upper = lax.broadcasted_iota(jnp.int32, (B, B), 0) < BLK
     left = lax.broadcasted_iota(jnp.int32, (B, B), 1) < BLK
     errors, scales = [], []
-    for b in range(NB):
-        block = jnp.where(upper == left, mat[b, b], 0.0)
+    for b in range(NB // 2):
+        block = jnp.where(upper == left, mat[start + b, start + b], 0.0)
         middle = jnp.where(identity, block, 0.0)
         row = lax.rsqrt(jnp.sum(middle, axis=0, keepdims=True))
         column = lax.rsqrt(jnp.sum(middle, axis=1, keepdims=True))
@@ -425,15 +470,15 @@
     sums = [one + error for error in errors]
     errors = [times(error, error) for error in errors]
     for n in range(DOUBLINGS):
-        for b in range(NB):
+        for b in range(NB // 2):
             if n + 1 == DOUBLINGS:
                 sums[b] = sums[b] + times(sums[b], errors[b])
             else:
                 both = times(jnp.concatenate([errors[b], sums[b]], axis=0), errors[b])
                 errors[b] = both[:B]
                 sums[b] = sums[b] + both[B:]
-    for b in range(NB):
-        inverse[b] = sums[b] * scales[b]
+    for b in range(NB // 2):
+        inverse[start + b] = sums[b] * scales[b]
 
 
 def eliminate(mat, spare, right, columns, out):
@@ -655,12 +700,14 @@
     own_rows = tiles * BLK
     rows_total = own_rows * lax.axis_size("rows") * lax.axis_size("grp")
     ridge = rows_total / (2.0 * NC)
-    groups = 3 + 2 + 3 + 2 + 3 + 3
+    groups = 8 + 2 + 3 + 2 + 8 + 3
     job_space = [
         space(HALF, B),
         space(NZ - 1, SLAB, B),
         space(NY - 1, SLAB, B),
-        space(NX - 1, WIDE, B),
+        space(2, WIDE, B),
+        space(2, WIDE // 2, B),
+        space(2, WIDE // 2, B),
         space(NY, CELL + THIN1, B),
         space(NZ, CELL + THIN2, B),
         space(NY - 1, CELL + THIN1, B),

time: 82 us -> 78.9 us (0.962)
  Pallas kernels: 81.2 us -> 78.1 us
    pallas_call x1, Pallas kernels: 72.3 us -> 69.2 us  [body(): pl.pallas_call(lambda *refs: reduce_kernel(ridge, *refs), out_shape=(shap...]
where the time goes in v3:
time: 78.9 us; the launch traced here: 78.7 us
  Pallas kernels  78.1 us (99%)
    pallas_call x1, Pallas kernels, body(): pl.pallas_call(lambda *refs: reduce_kernel(ridge, *refs), out_shape=(shap...  69.2 us
    pallas_call x1, Pallas kernels, body(): pl.pallas_call(lambda *refs: solver_kernel(ridge, *refs), out_shape=(shap...  8.86 us

profile of v3, /device:TPU:1, one launch (start us, length us, event | category | flops | bytes accessed | tf_op | source)
XLA Modules:
  0.0 78.7 jit_solution(2670195955598548254)
XLA Ops:
  0.6 69.2 %shard_map.59 = (f32[4608,128]{1,0:T(8,128)S(1)}, bf16[1024,256]{1,0:T(8,128)(2,1)S(1)}, f32[8,8,128,128]{3,2,1,0:T(8,128)S(1)}, f32[8,128,128]{2,1,0:T(8,128)S(...) custom-call(bf16[2,128,256]{2,1,0:T(8,128)(2,1)} %bitcast.7, s32[4,4]{1,0:T(4,128)} %refs_1_.1, ...), custom_call_target="tpu_custom_call" | custom-call | tf_op jit(solution)/shard_map/pallas_call | solution.py:721
  69.9 8.9 %shard_map.60 = (f32[8,128]{1,0:T(8,128)}, f32[2,128]{1,0:T(2,128)}) custom-call(f32[36,128,128]{2,1,0:T(8,128)S(1)} %bitcast.6, bf16[1024,256]{1,0:T(8,128)(2,1)S(1)} %get-tuple-element.12.refs_1_, f32[8,8,128,128]{3,2,1,0:T(8,128)S(1)} %get-tuple-element.13.refs_2_, f32[8,128,128]{2,1,0:T(8,128)S(1)} %get-tuple-element.14.refs_3_, ...), custom_call_target="tpu_custom_call" | custom-call | tf_op jit(solution)/shard_map/pallas_call | solution.py:760

commit v4 on v3

--- a/solution.py
+++ b/solution.py
@@ -638,8 +638,7 @@
             mat[j, i] = block.T
 
 
-def apply_operator(blocks, ridge, vector, columns):
-    spread_columns(vector, columns)
+def apply_weighted(blocks, vector, columns):
     down = [jnp.zeros((8, B), jnp.float32)] * NB
     rows = []
     for i in range(NB):
@@ -652,35 +651,56 @@
                 if j != i:
                     across = across + block * vector[j : j + 1, :]
         rows.append(to_row(jnp.sum(across, axis=1, keepdims=True)))
-    total = [jnp.sum(part, axis=0, keepdims=True) + row for part, row in zip(down, rows)]
-    return pack(total) + ridge * vector
-
-
-def solver_kernel(ridge, blocks, dense_t, mat, inverse, side, begin, left, solution, fitted, spare, columns, first, second):
+    return pack([jnp.sum(part, axis=0, keepdims=True) + row for part, row in zip(down, rows)])
+
+
+def weighted_square(blocks, vector, columns):
+    total = jnp.zeros((8, B), jnp.float32)
+    twice = 2.0 * vector
+    for i in range(NB):
+        across = jnp.zeros((B, B), jnp.float32)
+        for j in range(NB):
+            if (i, j) in INDEX:
+                row = vector if i == j else twice
+                across = across + blocks[INDEX[i, j]] * row[j : j + 1, :]
+        total = total + block_rows(across, columns[i])
+    return jnp.sum(jnp.sum(total, axis=0, keepdims=True), axis=1, keepdims=True)
+
+
+def design_lines(dense_t, columns):
+    lines = []
+    for half in range(2):
+        acc = jnp.zeros((8, B), jnp.float32)
+        for j in range(NB):
+            part = dense_t[j * B : (j + 1) * B, half * B : (half + 1) * B].astype(jnp.float32)
+            acc = acc + block_rows(part, columns[j])
+        lines.append(jnp.sum(acc, axis=0, keepdims=True))
+    return lines
+
+
+def solver_kernel(
+    ridge, blocks, dense_t, mat, inverse, side, begin, left, solution, fitted, spare, columns, first, second
+):
     g = side[...]
     least = solve(mat, inverse, spare, columns, g, first, (begin[...], left[...]))
     z = first[...]
-    h = apply_operator(blocks, ridge, z, columns)
+    spread_columns(z, columns)
+    h = apply_weighted(blocks, z, columns) + ridge * z
+    first_lines = design_lines(dense_t, columns)
     gain = dot(g, z)
     length = gain / dot(z, h)
     rest = g - length * h
     solve(mat, inverse, spare, columns, rest, second, least=least)
     s = second[...]
     latest = dot(rest, s)
-    ratio = latest / gain
-    image = apply_operator(blocks, ridge, s, columns) + ratio * h
-    step = s + ratio * z
-    curve = dot(step, image)
-    x = length * z + jnp.where(curve > 0.0, latest / curve, 0.0) * step
-    solution[...] = x
-
-    spread_columns(x, columns)
+    step = s + (latest / gain) * z
+    spread_columns(step, columns)
+    curve = weighted_square(blocks, step, columns) + ridge * dot(step, step)
+    last_lines = design_lines(dense_t, columns)
+    further = jnp.where(curve > 0.0, latest / curve, 0.0)
+    solution[...] = length * z + further * step
     for half in range(2):
-        acc = jnp.zeros((8, B), jnp.float32)
-        for j in range(NB):
-            part = dense_t[j * B : (j + 1) * B, half * B : (half + 1) * B].astype(jnp.float32)
-            acc = acc + block_rows(part, columns[j])
-        fitted[half : half + 1, :] = jnp.sum(acc, axis=0, keepdims=True)
+        fitted[half : half + 1, :] = length * first_lines[half] + further * last_lines[half]
 
 
 def space(*shape):

time: 78.9 us -> 78.7 us (level)
  no operation moved by 1% of the time
where the time goes in v4:
time: 78.7 us; the launch traced here: 78.5 us
  Pallas kernels  77.9 us (99%)
    pallas_call x1, Pallas kernels, body(): pl.pallas_call(lambda *refs: reduce_kernel(ridge, *refs), out_shape=(shap...  69.2 us
    pallas_call x1, Pallas kernels, body(): pl.pallas_call(lambda *refs: solver_kernel(ridge, *refs), out_shape=(shap...  8.66 us

profile of v4, /device:TPU:1, one launch (start us, length us, event | category | flops | bytes accessed | tf_op | source)
XLA Modules:
  0.0 78.5 jit_solution(16253523096577448294)
XLA Ops:
  0.6 69.2 %shard_map.59 = (f32[4608,128]{1,0:T(8,128)S(1)}, bf16[1024,256]{1,0:T(8,128)(2,1)S(1)}, f32[8,8,128,128]{3,2,1,0:T(8,128)S(1)}, f32[8,128,128]{2,1,0:T(8,128)S(...) custom-call(bf16[2,128,256]{2,1,0:T(8,128)(2,1)} %bitcast.7, s32[4,4]{1,0:T(4,128)} %refs_1_.1, ...), custom_call_target="tpu_custom_call" | custom-call | tf_op jit(solution)/shard_map/pallas_call | solution.py:741
  69.9 8.7 %shard_map.60 = (f32[8,128]{1,0:T(8,128)}, f32[2,128]{1,0:T(2,128)}) custom-call(f32[36,128,128]{2,1,0:T(8,128)S(1)} %bitcast.6, bf16[1024,256]{1,0:T(8,128)(2,1)S(1)} %get-tuple-element.12.refs_1_, f32[8,8,128,128]{3,2,1,0:T(8,128)S(1)} %get-tuple-element.13.refs_2_, f32[8,128,128]{2,1,0:T(8,128)S(1)} %get-tuple-element.14.refs_3_, ...), custom_call_target="tpu_custom_call" | custom-call | tf_op jit(solution)/shard_map/pallas_call | solution.py:780
